TPU v7x, 256 devices: a whole 4x4x8 slice. The times are simulated.
256 devices in a mesh: img: 32 (over z_hi, y, core), txt: 8 (over x, z_lo).
Axes of the slice: x: 4, y: 4, z: 8 (z_hi: 4, z_lo: 2; z = z_hi * 2 + z_lo), core: 2. Of those that a mesh axis runs over, the one named last changes fastest.
Arguments:
- image_feats: bfloat16 [20480, 1152], P(('img', 'txt')), may hold values from -0.59765625 to 0.59765625
- text_feats: bfloat16 [20480, 1152], P(('img', 'txt')), may hold values from -0.59765625 to 0.59765625
- image_gain: float32 [1152], replicated, may hold values from 0.5 to 2
- text_gain: float32 [1152], replicated, may hold values from 0.5 to 2
Outputs:
- grad_image: bfloat16 [20480, 1152], P(('img', 'txt'))
- grad_text: bfloat16 [20480, 1152], P(('img', 'txt'))
All inputs are finite; a program needn't handle non-finite values.
Results may differ from a plain program's by a relative error of at most 0.007.
Values may be sent and summed in bfloat16 or wider, within the bound.
A program may use at most 64 MiB of HBM per device.

v0:
```python
import math

import jax
import jax.numpy as jnp
from jax import lax
from jax.sharding import PartitionSpec as P

EPSILON = 1e-06
BIAS_VALUE = -8.0


def embedding(feats, gain):
    centre = feats - jnp.mean(feats, axis=-1, keepdims=True)
    spread = jnp.mean(centre * centre, axis=-1, keepdims=True)
    normed = centre * lax.rsqrt(spread + EPSILON) * gain
    energy = jnp.mean(normed * normed, axis=-1, keepdims=True)
    return normed * lax.rsqrt(energy + EPSILON) / math.sqrt(feats.shape[-1])


def local(image_feats, text_feats, image_gain, text_gain):
    row_count = text_feats.shape[0]
    width = text_feats.shape[1]
    image_unit, image_back = jax.vjp(
        lambda values: embedding(values, image_gain), image_feats.astype(jnp.float32)
    )
    text_unit, text_back = jax.vjp(
        lambda values: embedding(values, text_gain), text_feats.astype(jnp.float32)
    )
    image_emb = image_unit.astype(jnp.bfloat16)
    text_emb = text_unit.astype(jnp.bfloat16)
    staying, moving = (image_emb, text_emb)
    group_rows = lax.all_gather(staying, "txt", axis=0, tiled=True)
    own_img = lax.axis_index("img")
    own_txt = lax.axis_index("txt")
    text_ways = lax.axis_size("txt")
    logit_scale = 2.0 * math.sqrt(width)
    group_index = own_img * (text_ways * row_count) + jnp.arange(
        group_rows.shape[0], dtype=jnp.int32
    )
    segment = lax.all_gather(moving, "img", axis=0, tiled=True)
    length = segment.shape[0]
    positions = jnp.arange(length, dtype=jnp.int32)
    moving_index = (
        positions // row_count * text_ways + own_txt
    ) * row_count + positions % row_count
    logits = (
        logit_scale
        * lax.dot_general(
            segment, group_rows, (((1,), (1,)), ((), ())), preferred_element_type=jnp.float32
        )
        + BIAS_VALUE
    )
    matches = (moving_index[:, None] == group_index[None, :]).astype(jnp.float32)
    weights_tile = (logit_scale * (jax.nn.sigmoid(logits) - matches)).astype(jnp.bfloat16)
    d_group = lax.dot_general(
        weights_tile, segment, (((0,), (0,)), ((), ())), preferred_element_type=jnp.float32
    )
    moving_term = jnp.dot(weights_tile, group_rows, preferred_element_type=jnp.float32)
    d_moving = moving_term
    d_group, d_moving = (d_group, d_moving)
    moving_cot = lax.psum_scatter(d_moving, "img", scatter_dimension=0, tiled=True)
    staying_cot = lax.psum_scatter(d_group, "txt", scatter_dimension=0, tiled=True)
    image_cot, text_cot = (staying_cot, moving_cot)
    grad_image = image_back(image_cot)[0].astype(jnp.bfloat16)
    grad_text = text_back(text_cot)[0].astype(jnp.bfloat16)
    return (grad_image, grad_text)


def solution(mesh):
    placed = (P(("img", "txt"), None), P(("img", "txt"), None), P(), P())
    return jax.shard_map(
        local,
        mesh=mesh,
        in_specs=placed,
        out_specs=(P(("img", "txt"), None), P(("img", "txt"), None)),
        check_vma=False,
    )
```

profile of v0, /device:TPU:2, one launch (start us, length us, event | category | flops | bytes accessed | tf_op | source)
XLA Modules:
  0.0 369.9 jit_solution(6982767176872682384)
XLA Ops:
  7.2 0.0 all-gather.5.cloned.1.call-start
  7.2 1.0 convert_reduce_fusion
  8.3 1.1 fusion.19
  9.4 1.2 fusion.25
  10.6 1.8 fusion.27
  12.4 0.0 all-gather.5.cloned.1.call-update
  12.5 0.0 all-gather.3.cloned.1.call-start
  12.5 1.0 convert_reduce_fusion.1
  13.6 1.1 fusion.8
  14.7 1.2 fusion.14
  15.9 1.8 fusion.16
  17.7 0.0 all-gather.3.cloned.1.call-update
  17.8 0.0 reduce-scatter.3.cloned.1.call-start
  17.9 40.9 %all-gather.5.cloned.1.call-done = bf16[640,1152]{1,0:T(8,128)(2,1)} async-done(((bf16[80,1152]{1,0:T(8,128)(2,1)}), bf16[640,1152]{1,0:T(8,128)(2,1)}) %all-gather.5.cloned.1.call-update) | async-done | bytes 1474576 | tf_op jit(solution)/shard_map/all_gather | solution.py:32
  58.8 71.3 %all-gather.3.cloned.1.call-done = bf16[2560,1152]{1,0:T(8,128)(2,1)} async-done(((bf16[80,1152]{1,0:T(8,128)(2,1)}), bf16[2560,1152]{1,0:T(8,128)(2,1)}) %all-gather.3.cloned.1.call-update) | async-done | bytes 5898256 | tf_op jit(solution)/shard_map/all_gather | solution.py:40
  130.1 8.4 %multiply_convert_fusion = bf16[2560,640]{1,0:T(8,128)(2,1)S(1)} fusion(bf16[2560,1152]{1,0:T(8,128)(2,1)} %all-gather.3.cloned.1.call-done, bf16[640,1152]{1,0:T(8,128)(2,1)} %all-gather.5.cloned.1.call-done, s32[640]{0:T(1024)S(1)} %iota_add_fusion, s32[2560]{0:T(1024)S(1)} %fusion.41), kind=kOutput, calls=%fused_computation | convolution fusion | flops 3791257600 | bytes 10662400 | tf_op jit(solution)/shard_map/dot_general | solution.py:48
  138.6 1.8 copy-done.6
  140.4 6.0 %fusion.49 = f32[640,1152]{1,0:T(8,128)} fusion(bf16[2560,640]{1,0:T(8,128)(2,1)S(1)} %multiply_convert_fusion, bf16[2560,1152]{1,0:T(8,128)(2,1)S(1)} %copy-done.4), kind=kOutput, calls=%fused_computation.79 | convolution fusion | flops 3774873600 | bytes 12124160 | tf_op jit(solution)/shard_map/dot_general | solution.py:55
  146.4 0.0 reduce-scatter.3.cloned.1.call-update
  146.4 0.2 reduce-scatter.5.cloned.1.call-start
  146.7 9.3 %fusion.50 = f32[2560,1152]{1,0:T(8,128)} fusion(bf16[2560,640]{1,0:T(8,128)(2,1)} %copy-done.6, bf16[640,1152]{1,0:T(8,128)(2,1)S(1)} %copy-done.5), kind=kOutput, calls=%fused_computation.80 | convolution fusion | flops 3774873600 | bytes 16547840 | tf_op jit(solution)/shard_map/dot_general | solution.py:58
  156.0 0.0 reduce-scatter.5.cloned.1.call-update
  156.0 58.0 %reduce-scatter.3.cloned.1.call-done = f32[80,1152]{1,0:T(8,128)} async-done(((f32[640,1152]{1,0:T(8,128)}), f32[80,1152]{1,0:T(8,128)}) %reduce-scatter.3.cloned.1.call-update) | async-done | bytes 368656 | tf_op jit(solution)/shard_map/reduce_scatter | solution.py:62
  214.0 1.3 fusion.28
  215.2 1.3 fusion.29
  216.6 1.4 fusion.48
  218.0 0.8 add_convert_fusion.1
  218.7 139.8 %reduce-scatter.5.cloned.1.call-done = f32[80,1152]{1,0:T(8,128)} async-done(((f32[2560,1152]{1,0:T(8,128)}), f32[80,1152]{1,0:T(8,128)}) %reduce-scatter.5.cloned.1.call-update) | async-done | bytes 368656 | tf_op jit(solution)/shard_map/reduce_scatter | solution.py:61
  358.6 1.2 fusion.17
  359.8 1.3 fusion.18
  361.2 1.4 fusion.47
  362.6 0.8 add_convert_fusion
  (27 shorter events, 0.1 us)
Async XLA Ops:
  7.2 51.6 %all-gather.5.cloned.1.call-start = ((), (), s32[]{:S(2)}) async-start(), calls=%async_computation.3 | async-start | bytes 1658880 | tf_op jit(solution)/shard_map/all_gather | solution.py:32
  12.5 117.6 %all-gather.3.cloned.1.call-start = ((), (), s32[]{:S(2)}) async-start(), calls=%async_computation.2 | async-start | bytes 6082560 | tf_op jit(solution)/shard_map/all_gather | solution.py:40
  17.8 196.2 %reduce-scatter.3.cloned.1.call-start = ((), (), s32[]{:S(2)}) async-start(), calls=%async_computation.4 | async-start | bytes 3317760 | tf_op jit(solution)/shard_map/reduce_scatter | solution.py:62
  130.1 10.3 %copy-start.4 = (bf16[2560,1152]{1,0:T(8,128)(2,1)S(1)}, bf16[2560,1152]{1,0:T(8,128)(2,1)}, u32[]{:S(2)}) copy-start(bf16[2560,1152]{1,0:T(8,128)(2,1)} %all-gather.3.cloned.1.call-done) | copy-start | bytes 17694724
  138.6 1.8 copy-start.6
  140.4 6.3 %copy-start.5 = (bf16[640,1152]{1,0:T(8,128)(2,1)S(1)}, bf16[640,1152]{1,0:T(8,128)(2,1)}, u32[]{:S(2)}) copy-start(bf16[640,1152]{1,0:T(8,128)(2,1)} %all-gather.5.cloned.1.call-done) | copy-start | bytes 4423684
  146.4 212.1 %reduce-scatter.5.cloned.1.call-start = ((), (), s32[]{:S(2)}) async-start(), calls=%async_computation.5 | async-start | bytes 12165120 | tf_op jit(solution)/shard_map/reduce_scatter | solution.py:61
  155.9 58.0 %copy-start = (bf16[80,1152]{1,0:T(8,128)(2,1)S(1)}, bf16[80,1152]{1,0:T(8,128)(2,1)}, u32[]{:S(2)}) copy-start(bf16[80,1152]{1,0:T(8,128)(2,1)} %param.4) | copy-start | bytes 552964
  156.0 58.0 %copy-start.2 = (f32[1152]{0:T(1024)S(1)}, f32[1152]{0:T(1024)}, u32[]{:S(2)}) copy-start(f32[1152]{0:T(1024)} %param.6) | copy-start | bytes 13828
  156.0 202.6 %copy-start.1 = (bf16[80,1152]{1,0:T(8,128)(2,1)S(1)}, bf16[80,1152]{1,0:T(8,128)(2,1)}, u32[]{:S(2)}) copy-start(bf16[80,1152]{1,0:T(8,128)(2,1)} %param.5) | copy-start | bytes 552964
  156.0 202.6 %copy-start.3 = (f32[1152]{0:T(1024)S(1)}, f32[1152]{0:T(1024)}, u32[]{:S(2)}) copy-start(f32[1152]{0:T(1024)} %param.7) | copy-start | bytes 13828
Sparse Core Ops, SparseCore 0:
  12.6 46.1 all-gather.4
  62.0 68.0 all-gather.2
  146.6 67.3 reduce-scatter.2
  218.5 140.0 reduce-scatter.4
where the time goes:
time: 370 us
  waiting for transfers between devices  310 us (84%)
  matrix products  23.8 us (6%)
  other arithmetic  19.9 us (5%)
  between operations  14 us (4%)
    reduce_scatter x1, waiting for transfers between devices, local(): lax.psum_scatter(d_moving, 'img', scatter_dimension=0, tiled=True)  140 us
    all_gather x1, waiting for transfers between devices, local(): segment = lax.all_gather(moving, 'img', axis=0, tiled=True)  71.3 us
    reduce_scatter x1, waiting for transfers between devices, local(): lax.psum_scatter(d_group, 'txt', scatter_dimension=0, tiled=True)  58 us
    all_gather x1, waiting for transfers between devices, local(): group_rows = lax.all_gather(staying, 'txt', axis=0, tiled=True)  40.9 us
    dot_general x1, matrix products, local(): jnp.dot(weights_tile, group_rows, preferred_element_type=jnp.float32)  9.27 us
    dot_general x1, matrix products, local(): lax.dot_general(segment, group_rows, (((1,), (1,)), ((), ())), preferred_...  8.44 us
  transfers between devices with their start and end apart: 4, of which 4 were waited for; matrix products, arithmetic and copies ran while one was open for 5% of the time, Pallas kernels for 0%

commit v1 on v0

v1 whole, which is shorter than its diff:
```python
import math

import jax
import jax.numpy as jnp
from jax import lax
from jax.experimental import pallas as pl
from jax.experimental.pallas import tpu as pltpu
from jax.sharding import PartitionSpec as P

MESH = pl.DeviceIdType.MESH
EPSILON = 1e-06
BIAS_VALUE = -8.0
ROWS = 80
WIDTH = 1152
TOTAL = 16 * ROWS
SCALE = 2.0 * math.sqrt(WIDTH)
LOG2E = math.log2(math.e)
TILE = 256
F32 = jnp.float32
BF16 = jnp.bfloat16

HALVES = ((0, 48), (48, 32))

T_ORDER = [(dp, dq) for dq in (0, 1, 3, 2) for dp in (0, 1, 3, 2)]
Z_ORDER = (0, 1, -1, 2, -2, 3, -3, 4)


def t_row(dp, dq):
    return T_ORDER.index((dp % 4, dq % 4)) * ROWS


def wrap_z(dz):
    return (dz + 3) % 8 - 3


def i_row(dz, dc):
    return (2 * Z_ORDER.index(wrap_z(dz)) + dc) * ROWS


def mean(values):
    return jnp.sum(values, axis=-1, keepdims=True) * (1.0 / WIDTH)


def embed(feats_ref, gain_ref, normed_ref, r1_ref, r2_ref):
    feats = feats_ref[...].astype(F32)
    centre = feats - mean(feats)
    r1 = lax.rsqrt(mean(centre * centre) + EPSILON)
    normed = centre * r1
    scaled = normed * gain_ref[...]
    r2 = lax.rsqrt(mean(scaled * scaled) + EPSILON)
    normed_ref[...] = normed
    r1_ref[...] = r1
    r2_ref[...] = r2
    return (scaled * (r2 * (1.0 / math.sqrt(WIDTH)))).astype(BF16)


def embed_back(cot, gain_ref, normed_ref, r1_ref, r2_ref):
    normed, r1, r2, gain = normed_ref[...], r1_ref[...], r2_ref[...], gain_ref[...]
    scaled = normed * gain
    d_scaled = (cot - scaled * (r2 * r2 * mean(cot * scaled))) * (r2 * (1.0 / math.sqrt(WIDTH)))
    d_normed = d_scaled * gain
    d_centre = (d_normed - normed * mean(d_normed * normed)) * r1
    return (d_centre - mean(d_centre)).astype(BF16)


class Net:
    def __init__(self, send_sems, recv_sems):
        self.send_sems, self.recv_sems = send_sems, recv_sems
        self.copies = {}
        i, t = lax.axis_index("img"), lax.axis_index("txt")
        c, y, x = i % 2, (i // 2) % 4, t // 2
        z = (i // 8) * 2 + t % 2

        def place(x, y, z, c):
            x, y, z = (x + 4) % 4, (y + 4) % 4, (z + 8) % 8
            return (((z // 2) * 4 + y) * 2 + c, x * 2 + z % 2)

        s = 1 - 2 * c
        self.device = {
            "p+": place(x + (1 - c), y + c, z, c),
            "p-": place(x - (1 - c), y - c, z, c),
            "q+": place(x + c, y + (1 - c), z, c),
            "q-": place(x - c, y - (1 - c), z, c),
            "z+": place(x, y, z + s, c),
            "z-": place(x, y, z - s, c),
            "c": place(x, y, z, 1 - c),
        }

    def greet(self):
        barrier = pltpu.get_barrier_semaphore()
        for device in self.device.values():
            pl.semaphore_signal(barrier, inc=1, device_id=device, device_id_type=MESH)

    def greeted(self):
        pl.semaphore_wait(pltpu.get_barrier_semaphore(), len(self.device))

    def send(self, key, src, dst, way):
        number = len(self.copies)
        assert key not in self.copies
        copy = pltpu.make_async_remote_copy(
            src_ref=src,
            dst_ref=dst,
            send_sem=self.send_sems.at[number],
            recv_sem=self.recv_sems.at[number],
            device_id=self.device[way],
            device_id_type=MESH,
        )
        copy.start()
        self.copies[key] = copy

    def arrived(self, key):
        self.copies[key].wait_recv()

    def finish(self):
        for copy in self.copies.values():
            copy.wait_send()


N_COPIES = 160
T_SLOTS = 16
I_SLOTS = 16


def kernel(
    image_ref, text_ref, image_gain_ref, text_gain_ref, image_out, text_out,
    tbuf, ibuf, w, wt, dtext, dimage, tsend, trecv, isend, irecv, csend, crecv,
    inorm, ir1, ir2, tnorm, tr1, tr2, send_sems, recv_sems,
):
    net = Net(send_sems, recv_sems)
    net.greet()

    def send_t(dp, dq, part, way):
        first, size = part
        step = 1 if way[1] == "+" else -1
        there = (dp - step, dq) if way[0] == "p" else (dp, dq - step)
        there = (there[0] % 4, there[1] % 4)
        net.send(
            ("tg", there, first),
            tbuf.at[pl.ds(t_row(dp, dq) + first, size)],
            tbuf.at[pl.ds(t_row(*there) + first, size)],
            way,
        )

    def wait_t(dp, dq, part):
        net.arrived(("tg", (dp % 4, dq % 4), part[0]))

    def send_z(dz, part, way):
        first, size = part
        there = wrap_z(dz - 1 if way == "z+" else dz + 1)
        net.send(
            ("ig", there, 0, first),
            ibuf.at[pl.ds(i_row(dz, 0) + first, size)],
            ibuf.at[pl.ds(i_row(there, 0) + first, size)],
            way,
        )

    def send_c(dz, part):
        first, size = part
        there = wrap_z(-dz)
        net.send(
            ("ig", there, 1, first),
            ibuf.at[pl.ds(i_row(dz, 0) + first, size)],
            ibuf.at[pl.ds(i_row(there, 1) + first, size)],
            "c",
        )

    def wait_i(dz, dc, part):
        net.arrived(("ig", dz, dc, part[0]))

    def tile(a, b, own=False):
        ta, ib = pl.ds(a * TILE, TILE), pl.ds(b * TILE, TILE)
        if not isinstance(a, int):
            ta = pl.ds(pl.multiple_of(a * TILE, TILE), TILE)
        if not isinstance(b, int):
            ib = pl.ds(pl.multiple_of(b * TILE, TILE), TILE)
        dots = lax.dot_general(
            tbuf[ta, :], ibuf[ib, :], (((1,), (1,)), ((), ())), preferred_element_type=F32
        )
        weights = SCALE / (1.0 + jnp.exp2(dots * (-SCALE * LOG2E) - BIAS_VALUE * LOG2E))
        if own:
            row = lax.broadcasted_iota(jnp.int32, (TILE, TILE), 0)
            column = lax.broadcasted_iota(jnp.int32, (TILE, TILE), 1)
            weights = weights - jnp.where((row == column) & (row < ROWS), SCALE, 0.0)
        w[ta, ib] = weights.astype(BF16)
        wt[ib, ta] = weights.T.astype(BF16)

    def tiles(first_a, first_b, count_a, count_b):
        @pl.loop(0, count_a * count_b)
        def _(k):
            tile(first_a + k // count_b, first_b + k % count_b)

    whole = (0, ROWS)
    tbuf[0:ROWS, :] = embed(text_ref, text_gain_ref, tnorm, tr1, tr2)
    net.greeted()
    for part in HALVES:
        for way in ("p+", "p-", "q+", "q-"):
            send_t(0, 0, part, way)
    ibuf[0:ROWS, :] = embed(image_ref, image_gain_ref, inorm, ir1, ir2)
    for part in HALVES:
        for way in ("z+", "z-"):
            send_z(0, part, way)
    send_c(0, whole)

    for k, part in enumerate(HALVES):
        wait_t(-1, 0, part)
        if k == 0:
            send_t(-1, 0, part, "p+")
        send_t(-1, 0, part, "q+")
        send_t(-1, 0, part, "q-")
        wait_t(1, 0, part)
        if k == 1:
            send_t(1, 0, part, "p-")
        send_t(1, 0, part, "q+")
        send_t(1, 0, part, "q-")
        wait_i(-1, 0, part)
        send_z(-1, part, "z+")
        wait_i(1, 0, part)
        send_z(1, part, "z-")
    send_c(1, whole)
    send_c(-1, whole)
    for k, part in enumerate(HALVES):
        wait_t(0, -1, part)
        send_t(0, -1, part, "q+")
        wait_t(0, 1, part)
        wait_t(2, 0, part)
        send_t(2, 0, part, "q+")
        send_t(2, 0, part, "q-")
        wait_i(-2, 0, part)
        send_z(-2, part, "z+")
        wait_i(2, 0, part)
        send_z(2, part, "z-")
    send_c(2, whole)
    send_c(-2, whole)
    wait_i(0, 1, whole)
    wait_i(1, 1, whole)
    wait_i(-1, 1, whole)
    tile(0, 0, own=True)
    for part in HALVES:
        wait_t(1, -1, part)
        send_t(1, -1, part, "q+")
        wait_t(-1, 1, part)
        send_t(-1, 1, part, "q-")
        wait_t(1, 1, part)
        wait_t(-1, -1, part)
        wait_i(-3, 0, part)
        send_z(-3, part, "z+")
        wait_i(3, 0, part)
    send_c(3, whole)
    send_c(-3, whole)
    wait_i(2, 1, whole)
    wait_i(-2, 1, whole)
    tile(0, 1)
    tile(0, 2)
    for part in HALVES:
        wait_t(2, 1, part)
        send_t(2, 1, part, "q-")
        wait_t(2, -1, part)
    tiles(1, 0, 2, 3)
    for part in HALVES:
        wait_i(4, 0, part)
    send_c(4, whole)
    wait_i(3, 1, whole)
    wait_i(-3, 1, whole)
    tiles(0, 3, 3, 1)
    for part in HALVES:
        for dp in (0, 1, -1, 2):
            wait_t(dp, 2, part)
    tiles(3, 0, 2, 4)
    wait_i(4, 1, whole)
    tiles(0, 4, 5, 1)

    def text_rows(dq):
        rows = pl.ds(t_row(0, dq), 4 * ROWS)
        dtext[rows, :] = jnp.dot(w[rows, :], ibuf[...], preferred_element_type=F32)

    def image_rows(first, count):
        rows = pl.ds(first * ROWS, count * ROWS)
        dimage[rows, :] = jnp.dot(wt[rows, :], tbuf[...], preferred_element_type=F32)

    slots = {}

    def slot(kind, key):
        group = slots.setdefault(kind, {})
        return group.setdefault(key, len(group))

    def reduce_t(dp, dq, part, way, takes):
        first, size = part
        step = 1 if way[1] == "+" else -1
        there = (dp - step, dq) if way[0] == "p" else (dp, dq - step)
        key = (there[0] % 4, there[1] % 4, way)
        total = dtext[pl.ds(t_row(dp, dq) + first, size), :]
        total = taken_t(total, dp, dq, part, takes)
        out = tsend.at[slot("t", key), pl.ds(first, size)]
        out[...] = total.astype(BF16)
        net.send(("tr", key, first), out, trecv.at[slot("t", key), pl.ds(first, size)], way)

    def taken_t(total, dp, dq, part, takes):
        first, size = part
        for way in takes:
            key = (dp % 4, dq % 4, way)
            net.arrived(("tr", key, first))
            total = total + trecv[slot("t", key), pl.ds(first, size), :].astype(F32)
        return total

    def swap(dz):
        out = csend.at[Z_ORDER.index(dz)]
        out[...] = dimage[pl.ds(i_row(dz, 1), ROWS), :].astype(BF16)
        there = Z_ORDER.index(wrap_z(-dz))
        net.send(("cr", wrap_z(-dz)), out, crecv.at[there], "c")

    def swapped(dz):
        net.arrived(("cr", dz))
        rows = pl.ds(i_row(dz, 0), ROWS)
        dimage[rows, :] = dimage[rows, :] + crecv[Z_ORDER.index(dz)].astype(F32)

    def taken_i(total, dz, part, takes):
        first, size = part
        for way in takes:
            key = (dz, way)
            net.arrived(("ir", key, first))
            total = total + irecv[slot("i", key), pl.ds(first, size), :].astype(F32)
        return total

    def reduce_i(dz, part, way, takes):
        first, size = part
        total = taken_i(dimage[pl.ds(i_row(dz, 0) + first, size), :], dz, part, takes)
        key = (wrap_z(dz - 1 if way == "z+" else dz + 1), way)
        out = isend.at[slot("i", key), pl.ds(first, size)]
        out[...] = total.astype(BF16)
        net.send(("ir", key, first), out, irecv.at[slot("i", key), pl.ds(first, size)], way)

    image_rows(10, 6)
    for dz in (4, 3, -3):
        swap(dz)
    text_rows(2)
    for dp, way in ((2, "q+"), (1, "q-"), (0, "q+"), (-1, "q-")):
        reduce_t(dp, 2, whole, way, ())
    for dz in (4, 3, -3):
        swapped(dz)
    for part in HALVES:
        reduce_i(4, part, "z+", ())
        reduce_i(-3, part, "z-", ())
    text_rows(1)
    for dp in (1, -1):
        reduce_t(dp, 1, whole, "q+", ())
    text_rows(-1)
    for dp in (2, 0):
        reduce_t(dp, -1, whole, "q-", ())
    image_rows(6, 4)
    for dz in (2, -2):
        swap(dz)
    reduce_t(2, 1, whole, "q+", ("q+",))
    reduce_t(1, -1, whole, "q-", ("q-",))
    for dz in (2, -2):
        swapped(dz)
    for part in HALVES:
        reduce_i(3, part, "z+", ("z+",))
        reduce_i(-2, part, "z-", ("z-",))
    reduce_t(0, 1, whole, "q+", ("q+",))
    reduce_t(-1, -1, whole, "q-", ("q-",))
    image_rows(2, 4)
    for dz in (1, -1):
        swap(dz)
    text_rows(0)
    for part in HALVES:
        reduce_i(2, part, "z+", ("z+",))
    for dz in (1, -1):
        swapped(dz)
    for part in HALVES:
        reduce_i(-1, part, "z-", ("z-",))
    image_rows(0, 2)
    swap(0)

    def join(dp):
        rows = pl.ds(t_row(dp, 0), ROWS)
        dtext[rows, :] = taken_t(dtext[rows, :], dp, 0, whole, ("q+", "q-"))

    join(2)
    reduce_t(2, 0, HALVES[0], "p+", ())
    reduce_t(2, 0, HALVES[1], "p-", ())
    for part in HALVES:
        reduce_i(1, part, "z+", ("z+",))
    join(1)
    reduce_t(1, 0, HALVES[1], "p+", ())
    join(-1)
    reduce_t(-1, 0, HALVES[0], "p-", ())
    swapped(0)
    join(0)
    reduce_t(1, 0, HALVES[0], "p+", ("p+",))
    reduce_t(-1, 0, HALVES[1], "p-", ("p-",))
    total = dimage[0:ROWS, :]
    sums = [
        taken_i(total[first : first + size], 0, (first, size), ("z-", "z+"))
        for first, size in HALVES
    ]
    image_out[...] = embed_back(
        jnp.concatenate(sums, axis=0), image_gain_ref, inorm, ir1, ir2
    )
    total = dtext[0:ROWS, :]
    sums = [
        taken_t(total[first : first + size], 0, 0, (first, size), ("p+", "p-"))
        for first, size in HALVES
    ]
    text_out[...] = embed_back(jnp.concatenate(sums, axis=0), text_gain_ref, tnorm, tr1, tr2)
    net.finish()


def local(image_feats, text_feats, image_gain, text_gain):
    vmem = pl.BlockSpec(memory_space=pltpu.VMEM)
    block = jax.ShapeDtypeStruct((ROWS, WIDTH), BF16)
    flops = 6 * TOTAL * TOTAL * WIDTH
    return pl.pallas_call(
        kernel,
        out_shape=(block, block),
        in_specs=[vmem] * 4,
        out_specs=(vmem, vmem),
        scratch_shapes=[
            pltpu.VMEM((TOTAL, WIDTH), BF16),
            pltpu.VMEM((TOTAL, WIDTH), BF16),
            pltpu.VMEM((TOTAL, TOTAL), BF16),
            pltpu.VMEM((TOTAL, TOTAL), BF16),
            pltpu.VMEM((TOTAL, WIDTH), F32),
            pltpu.VMEM((TOTAL, WIDTH), F32),
            pltpu.VMEM((T_SLOTS, ROWS, WIDTH), BF16),
            pltpu.VMEM((T_SLOTS, ROWS, WIDTH), BF16),
            pltpu.VMEM((7, ROWS, WIDTH), BF16),
            pltpu.VMEM((7, ROWS, WIDTH), BF16),
            pltpu.VMEM((8, ROWS, WIDTH), BF16),
            pltpu.VMEM((8, ROWS, WIDTH), BF16),
            pltpu.VMEM((ROWS, WIDTH), F32),
            pltpu.VMEM((ROWS, 1), F32),
            pltpu.VMEM((ROWS, 1), F32),
            pltpu.VMEM((ROWS, WIDTH), F32),
            pltpu.VMEM((ROWS, 1), F32),
            pltpu.VMEM((ROWS, 1), F32),
            pltpu.SemaphoreType.DMA((N_COPIES,)),
            pltpu.SemaphoreType.DMA((N_COPIES,)),
        ],
        compiler_params=pltpu.CompilerParams(
            collective_id=0, has_side_effects=True, vmem_limit_bytes=56 * 2**20
        ),
        cost_estimate=pl.CostEstimate(
            flops=flops, bytes_accessed=4 * ROWS * WIDTH * 2, transcendentals=TOTAL * TOTAL
        ),
    )(image_feats, text_feats, image_gain.reshape(1, WIDTH), text_gain.reshape(1, WIDTH))


def solution(mesh):
    placed = (P(("img", "txt"), None), P(("img", "txt"), None), P(), P())
    return jax.shard_map(
        local,
        mesh=mesh,
        in_specs=placed,
        out_specs=(P(("img", "txt"), None), P(("img", "txt"), None)),
        check_vma=False,
    )
```

time: 370 us -> 71.8 us (0.19)
  waiting for transfers between devices: 310 us -> 0 us
  Pallas kernels: 0 us -> 66.8 us
  matrix products: 23.8 us -> 0 us
  other arithmetic: 19.9 us -> 0 us
  between operations: 14 us -> 0.66 us
    reduce_scatter x2 -> x0, waiting for transfers between devices: 198 us -> none  [the longest x1 140 us: local(): lax.psum_scatter(d_moving, 'img', scatter_dimension=0, tiled=True)]
    all_gather x2 -> x0, waiting for transfers between devices: 112 us -> none  [the longest x1 71.3 us: local(): segment = lax.all_gather(moving, 'img', axis=0, tiled=True)]
    pallas_call x0 -> x1, Pallas kernels: none -> 66.8 us  [local(): pl.pallas_call(kernel, out_shape=(block, block), in_specs=[vmem] * 4, out...]
    dot_general x3 -> x0, matrix products: 23.8 us -> none  [the longest x1 9.27 us: local(): jnp.dot(weights_tile, group_rows, preferred_element_type=jnp.float32)]
    reduce_sum x12 -> x0, other arithmetic: 14.7 us -> none  [the longest x4 4.83 us: embedding(): centre = feats - jnp.mean(feats, axis=-1, keepdims=True)]
    convert_element_type x4 -> x0, other arithmetic: 5.15 us -> none  [the longest x1 1.81 us: local(): image_emb = image_unit.astype(jnp.bfloat16)]
  transfers between devices with their start and end apart: 4 -> 0, of which waited for: 4 -> 0; matrix products, arithmetic and copies ran while one was open for 5% -> 0% of each run, Pallas kernels for 0% -> 0%
where the time goes in v1:
time: 71.8 us; the launch traced here: 71.7 us
  Pallas kernels  66.8 us (93%)
  local copies, waits for them, and re-layouts  4.22 us (6%)
    pallas_call x1, Pallas kernels, local(): pl.pallas_call(kernel, out_shape=(block, block), in_specs=[vmem] * 4, out...  66.8 us
    unnamed x6, local copies, waits for them, and re-layouts  2.33 us

profile of v1, /device:TPU:2, one launch (start us, length us, event | category | flops | bytes accessed | tf_op | source)
XLA Modules:
  0.0 71.7 jit_solution(14874538082800809037)
XLA Ops:
  0.6 0.0 copy-start.1
  0.6 1.3 %reshape.10.image_gain_ref = f32[1,1152]{1,0:T(1,128)} reshape(f32[1152]{0:T(1024)} %param.6) | data formatting | bytes 9216 | tf_op jit(solution)/shard_map/reshape | solution.py:445
  1.9 0.0 copy-done.1
  1.9 0.6 reshape.11.text_gain_ref
  2.5 66.8 %shard_map.59 = (bf16[80,1152]{1,0:T(8,128)(2,1)}, bf16[80,1152]{1,0:T(8,128)(2,1)}) custom-call(bf16[80,1152]{1,0:T(8,128)(2,1)} %image_ref.1, bf16[80,1152]{1,0:T(8,128)(2,1)} %text_ref.1, f32[1,1152]{1,0:T(1,128)} %reshape.10.image_gain_ref, f32[1,1152]{1,0:T(1,128)} %reshape.11.text_gain_ref), custom_call_target="tpu_custom_call" | custom-call | flops 11324620800 | bytes 737280 | tf_op jit(solution)/shard_map/pallas_call | solution.py:412
  69.3 0.0 copy-start
  69.3 1.6 %copy.8 = bf16[80,1152]{1,0:T(8,128)(2,1)} copy(bf16[80,1152]{1,0:T(8,128)(2,1)} %get-tuple-element.4) | data formatting | bytes 368640
  71.0 0.0 copy-done
  71.0 0.7 copy.9
Async XLA Ops:
  0.6 1.3 %copy-start.1 = (f32[1152]{0:T(1024)S(1)}, f32[1152]{0:T(1024)}, u32[]{:S(2)}) copy-start(f32[1152]{0:T(1024)} %param.7) | copy-start | bytes 13828
  69.3 1.7 %copy-start = (bf16[80,1152]{1,0:T(8,128)(2,1)S(1)}, bf16[80,1152]{1,0:T(8,128)(2,1)}, u32[]{:S(2)}) copy-start(bf16[80,1152]{1,0:T(8,128)(2,1)} %get-tuple-element.5) | copy-start | bytes 552964

commit v2 on v1

--- a/solution.py
+++ b/solution.py
@@ -116,7 +116,7 @@
             copy.wait_send()
 
 
-N_COPIES = 160
+N_COPIES = 111
 T_SLOTS = 16
 I_SLOTS = 16
 
@@ -124,9 +124,23 @@
 def kernel(
     image_ref, text_ref, image_gain_ref, text_gain_ref, image_out, text_out,
     tbuf, ibuf, w, wt, dtext, dimage, tsend, trecv, isend, irecv, csend, crecv,
-    inorm, ir1, ir2, tnorm, tr1, tr2, send_sems, recv_sems,
+    inorm, ir1, ir2, tnorm, tr1, tr2, image_in, text_in, image_gain_in, text_gain_in, in_sems,
+    send_sems, recv_sems,
 ):
     net = Net(send_sems, recv_sems)
+    staged = [
+        pltpu.make_async_copy(source, target, in_sems.at[k])
+        for k, (source, target) in enumerate(
+            (
+                (image_ref, image_in),
+                (image_gain_ref, image_gain_in),
+                (text_ref, text_in),
+                (text_gain_ref, text_gain_in),
+            )
+        )
+    ]
+    for copy in staged:
+        copy.start()
     net.greet()
 
     def send_t(dp, dq, part, way):
@@ -167,107 +181,110 @@
     def wait_i(dz, dc, part):
         net.arrived(("ig", dz, dc, part[0]))
 
-    def tile(a, b, own=False):
-        ta, ib = pl.ds(a * TILE, TILE), pl.ds(b * TILE, TILE)
-        if not isinstance(a, int):
-            ta = pl.ds(pl.multiple_of(a * TILE, TILE), TILE)
-        if not isinstance(b, int):
-            ib = pl.ds(pl.multiple_of(b * TILE, TILE), TILE)
+    def tile(first_t, count_t, first_i, count_i):
+        ts, im = pl.ds(first_t, count_t), pl.ds(first_i, count_i)
         dots = lax.dot_general(
-            tbuf[ta, :], ibuf[ib, :], (((1,), (1,)), ((), ())), preferred_element_type=F32
+            tbuf[ts, :], ibuf[im, :], (((1,), (1,)), ((), ())), preferred_element_type=F32
         )
         weights = SCALE / (1.0 + jnp.exp2(dots * (-SCALE * LOG2E) - BIAS_VALUE * LOG2E))
-        if own:
-            row = lax.broadcasted_iota(jnp.int32, (TILE, TILE), 0)
-            column = lax.broadcasted_iota(jnp.int32, (TILE, TILE), 1)
+        if first_t == 0 and first_i == 0:
+            row = lax.broadcasted_iota(jnp.int32, weights.shape, 0)
+            column = lax.broadcasted_iota(jnp.int32, weights.shape, 1)
             weights = weights - jnp.where((row == column) & (row < ROWS), SCALE, 0.0)
-        w[ta, ib] = weights.astype(BF16)
-        wt[ib, ta] = weights.T.astype(BF16)
-
-    def tiles(first_a, first_b, count_a, count_b):
-        @pl.loop(0, count_a * count_b)
-        def _(k):
-            tile(first_a + k // count_b, first_b + k % count_b)
+        weights = weights.astype(BF16)
+        w[ts, im] = weights
+        wt[im, ts] = weights.T
 
     whole = (0, ROWS)
-    tbuf[0:ROWS, :] = embed(text_ref, text_gain_ref, tnorm, tr1, tr2)
+    staged[0].wait()
+    staged[1].wait()
+    ibuf[0:ROWS, :] = embed(image_in, image_gain_in, inorm, ir1, ir2)
     net.greeted()
-    for part in HALVES:
-        for way in ("p+", "p-", "q+", "q-"):
-            send_t(0, 0, part, way)
-    ibuf[0:ROWS, :] = embed(image_ref, image_gain_ref, inorm, ir1, ir2)
     for part in HALVES:
         for way in ("z+", "z-"):
             send_z(0, part, way)
     send_c(0, whole)
+    staged[2].wait()
+    staged[3].wait()
+    tbuf[0:ROWS, :] = embed(text_in, text_gain_in, tnorm, tr1, tr2)
+    for ways in (("p+", "p-"), ("q+", "q-")):
+        for part in HALVES:
+            for way in ways:
+                send_t(0, 0, part, way)
 
     for k, part in enumerate(HALVES):
-        wait_t(-1, 0, part)
-        if k == 0:
-            send_t(-1, 0, part, "p+")
-        send_t(-1, 0, part, "q+")
-        send_t(-1, 0, part, "q-")
-        wait_t(1, 0, part)
-        if k == 1:
-            send_t(1, 0, part, "p-")
-        send_t(1, 0, part, "q+")
-        send_t(1, 0, part, "q-")
         wait_i(-1, 0, part)
         send_z(-1, part, "z+")
         wait_i(1, 0, part)
         send_z(1, part, "z-")
-    send_c(1, whole)
-    send_c(-1, whole)
+        wait_t(-1, 0, part)
+        if k == 0:
+            send_t(-1, 0, part, "p+")
+        wait_t(1, 0, part)
+        if k == 1:
+            send_t(1, 0, part, "p-")
+        for dp in (-1, 1):
+            send_t(dp, 0, part, "q+")
+            send_t(dp, 0, part, "q-")
+        send_c(1, part)
+        send_c(-1, part)
     for k, part in enumerate(HALVES):
         wait_t(0, -1, part)
         send_t(0, -1, part, "q+")
         wait_t(0, 1, part)
-        wait_t(2, 0, part)
-        send_t(2, 0, part, "q+")
-        send_t(2, 0, part, "q-")
         wait_i(-2, 0, part)
         send_z(-2, part, "z+")
         wait_i(2, 0, part)
         send_z(2, part, "z-")
-    send_c(2, whole)
-    send_c(-2, whole)
+        wait_t(2, 0, part)
+        send_t(2, 0, part, "q+")
+        send_t(2, 0, part, "q-")
+        send_c(2, part)
+        send_c(-2, part)
     wait_i(0, 1, whole)
-    wait_i(1, 1, whole)
-    wait_i(-1, 1, whole)
-    tile(0, 0, own=True)
+    for part in HALVES:
+        wait_i(1, 1, part)
+        wait_i(-1, 1, part)
+    tile(0, 256, 0, 256)
     for part in HALVES:
         wait_t(1, -1, part)
         send_t(1, -1, part, "q+")
         wait_t(-1, 1, part)
         send_t(-1, 1, part, "q-")
-        wait_t(1, 1, part)
-        wait_t(-1, -1, part)
         wait_i(-3, 0, part)
         send_z(-3, part, "z+")
         wait_i(3, 0, part)
-    send_c(3, whole)
-    send_c(-3, whole)
-    wait_i(2, 1, whole)
-    wait_i(-2, 1, whole)
-    tile(0, 1)
-    tile(0, 2)
+        send_c(3, part)
+        send_c(-3, part)
+        wait_t(1, 1, part)
+        wait_t(-1, -1, part)
+    for part in HALVES:
+        wait_i(2, 1, part)
+        wait_i(-2, 1, part)
+    tile(0, 256, 256, 512)
+    tile(256, 256, 0, 256)
     for part in HALVES:
         wait_t(2, 1, part)
         send_t(2, 1, part, "q-")
         wait_t(2, -1, part)
-    tiles(1, 0, 2, 3)
+    tile(256, 256, 256, 512)
     for part in HALVES:
         wait_i(4, 0, part)
-    send_c(4, whole)
-    wait_i(3, 1, whole)
-    wait_i(-3, 1, whole)
-    tiles(0, 3, 3, 1)
+        send_c(4, part)
+    tile(512, 256, 0, 768)
+    for part in HALVES:
+        wait_i(3, 1, part)
+        wait_i(-3, 1, part)
+    tile(0, 768, 768, 256)
+    for part in HALVES:
+        wait_i(4, 1, part)
+    tile(0, 768, 1024, 256)
     for part in HALVES:
         for dp in (0, 1, -1, 2):
             wait_t(dp, 2, part)
-    tiles(3, 0, 2, 4)
-    wait_i(4, 1, whole)
-    tiles(0, 4, 5, 1)
+    tile(768, 512, 768, 512)
+    tile(768, 512, 0, 256)
+    tile(768, 512, 256, 512)
 
     def text_rows(dq):
         rows = pl.ds(t_row(0, dq), 4 * ROWS)
@@ -329,90 +346,98 @@
         out[...] = total.astype(BF16)
         net.send(("ir", key, first), out, irecv.at[slot("i", key), pl.ds(first, size)], way)
 
+    def join(dp):
+        for first, size in HALVES:
+            rows = pl.ds(t_row(dp, 0) + first, size)
+            dtext[rows, :] = taken_t(dtext[rows, :], dp, 0, (first, size), ("q+", "q-"))
+
+    def pass_t(dp, dq, way, takes=()):
+        for part in HALVES:
+            reduce_t(dp, dq, part, way, takes)
+
+    def pass_i(dz, way, takes=()):
+        for part in HALVES:
+            reduce_i(dz, part, way, takes)
+
     image_rows(10, 6)
     for dz in (4, 3, -3):
         swap(dz)
     text_rows(2)
     for dp, way in ((2, "q+"), (1, "q-"), (0, "q+"), (-1, "q-")):
-        reduce_t(dp, 2, whole, way, ())
-    for dz in (4, 3, -3):
-        swapped(dz)
-    for part in HALVES:
-        reduce_i(4, part, "z+", ())
-        reduce_i(-3, part, "z-", ())
+        pass_t(dp, 2, way)
+    swapped(4)
+    pass_i(4, "z+")
+    swapped(-3)
+    pass_i(-3, "z-")
+    swapped(3)
     text_rows(1)
-    for dp in (1, -1):
-        reduce_t(dp, 1, whole, "q+", ())
+    pass_t(1, 1, "q+")
     text_rows(-1)
-    for dp in (2, 0):
-        reduce_t(dp, -1, whole, "q-", ())
+    pass_t(2, -1, "q-")
+    for part in HALVES:
+        reduce_t(2, 1, part, "q+", ("q+",))
+        reduce_t(1, -1, part, "q-", ("q-",))
+    pass_t(-1, 1, "q+")
+    pass_t(0, -1, "q-")
     image_rows(6, 4)
     for dz in (2, -2):
         swap(dz)
-    reduce_t(2, 1, whole, "q+", ("q+",))
-    reduce_t(1, -1, whole, "q-", ("q-",))
-    for dz in (2, -2):
-        swapped(dz)
-    for part in HALVES:
-        reduce_i(3, part, "z+", ("z+",))
-        reduce_i(-2, part, "z-", ("z-",))
-    reduce_t(0, 1, whole, "q+", ("q+",))
-    reduce_t(-1, -1, whole, "q-", ("q-",))
+    text_rows(0)
+    pass_i(3, "z+", ("z+",))
+    for part in HALVES:
+        reduce_t(0, 1, part, "q+", ("q+",))
+        reduce_t(-1, -1, part, "q-", ("q-",))
+    swapped(-2)
+    pass_i(-2, "z-", ("z-",))
+    swapped(2)
     image_rows(2, 4)
     for dz in (1, -1):
         swap(dz)
-    text_rows(0)
-    for part in HALVES:
-        reduce_i(2, part, "z+", ("z+",))
-    for dz in (1, -1):
-        swapped(dz)
-    for part in HALVES:
-        reduce_i(-1, part, "z-", ("z-",))
-    image_rows(0, 2)
-    swap(0)
-
-    def join(dp):
-        rows = pl.ds(t_row(dp, 0), ROWS)
-        dtext[rows, :] = taken_t(dtext[rows, :], dp, 0, whole, ("q+", "q-"))
-
     join(2)
     reduce_t(2, 0, HALVES[0], "p+", ())
     reduce_t(2, 0, HALVES[1], "p-", ())
-    for part in HALVES:
-        reduce_i(1, part, "z+", ("z+",))
+    pass_i(2, "z+", ("z+",))
+    swapped(-1)
+    pass_i(-1, "z-", ("z-",))
+    swapped(1)
+    image_rows(0, 2)
+    swap(0)
     join(1)
     reduce_t(1, 0, HALVES[1], "p+", ())
     join(-1)
     reduce_t(-1, 0, HALVES[0], "p-", ())
-    swapped(0)
-    join(0)
+    pass_i(1, "z+", ("z+",))
     reduce_t(1, 0, HALVES[0], "p+", ("p+",))
     reduce_t(-1, 0, HALVES[1], "p-", ("p-",))
+    join(0)
+    swapped(0)
+
+    total = dtext[0:ROWS, :]
+    sums = [
+        taken_t(total[first : first + size], 0, 0, (first, size), ("p+", "p-"))
+        for first, size in HALVES
+    ]
+    text_out[...] = embed_back(jnp.concatenate(sums, axis=0), text_gain_in, tnorm, tr1, tr2)
     total = dimage[0:ROWS, :]
     sums = [
         taken_i(total[first : first + size], 0, (first, size), ("z-", "z+"))
         for first, size in HALVES
     ]
     image_out[...] = embed_back(
-        jnp.concatenate(sums, axis=0), image_gain_ref, inorm, ir1, ir2
+        jnp.concatenate(sums, axis=0), image_gain_in, inorm, ir1, ir2
     )
-    total = dtext[0:ROWS, :]
-    sums = [
-        taken_t(total[first : first + size], 0, 0, (first, size), ("p+", "p-"))
-        for first, size in HALVES
-    ]
-    text_out[...] = embed_back(jnp.concatenate(sums, axis=0), text_gain_ref, tnorm, tr1, tr2)
+    assert len(net.copies) <= N_COPIES, len(net.copies)
     net.finish()
 
 
 def local(image_feats, text_feats, image_gain, text_gain):
     vmem = pl.BlockSpec(memory_space=pltpu.VMEM)
-    block = jax.ShapeDtypeStruct((ROWS, WIDTH), BF16)
+    block = pltpu.VMEM((ROWS, WIDTH), BF16)
     flops = 6 * TOTAL * TOTAL * WIDTH
     return pl.pallas_call(
         kernel,
         out_shape=(block, block),
-        in_specs=[vmem] * 4,
+        in_specs=[pl.BlockSpec(memory_space=pl.ANY)] * 4,
         out_specs=(vmem, vmem),
         scratch_shapes=[
             pltpu.VMEM((TOTAL, WIDTH), BF16),
@@ -433,6 +458,11 @@
             pltpu.VMEM((ROWS, WIDTH), F32),
             pltpu.VMEM((ROWS, 1), F32),
             pltpu.VMEM((ROWS, 1), F32),
+            pltpu.VMEM((ROWS, WIDTH), BF16),
+            pltpu.VMEM((ROWS, WIDTH), BF16),
+            pltpu.VMEM((WIDTH,), F32),
+            pltpu.VMEM((WIDTH,), F32),
+            pltpu.SemaphoreType.DMA((4,)),
             pltpu.SemaphoreType.DMA((N_COPIES,)),
             pltpu.SemaphoreType.DMA((N_COPIES,)),
         ],
@@ -442,7 +472,7 @@
         cost_estimate=pl.CostEstimate(
             flops=flops, bytes_accessed=4 * ROWS * WIDTH * 2, transcendentals=TOTAL * TOTAL
         ),
-    )(image_feats, text_feats, image_gain.reshape(1, WIDTH), text_gain.reshape(1, WIDTH))
+    )(image_feats, text_feats, image_gain, text_gain)
 
 
 def solution(mesh):

time: 71.8 us -> 63.5 us (0.88); the launches traced: 71.7 us -> 62.6 us
  Pallas kernels: 66.8 us -> 60.6 us
  local copies, waits for them, and re-layouts: 4.22 us -> 1.35 us
    pallas_call x1, Pallas kernels: 66.8 us -> 60.6 us  [local(): pl.pallas_call(kernel, out_shape=(block, block), in_specs=[pl.BlockSpec(m...]
    reshape x2 -> x0, local copies, waits for them, and re-layouts: 1.89 us -> none  [the longest x1 1.3 us: local(): image_gain.reshape(1, WIDTH)]
    unnamed x6 -> x2, local copies, waits for them, and re-layouts: 2.33 us -> 1.35 us
where the time goes in v2:
time: 63.5 us; the launch traced here: 62.6 us
  Pallas kernels  60.6 us (95%)
  local copies, waits for them, and re-layouts  1.35 us (2%)
  between operations  0.64 us (1%)
    pallas_call x1, Pallas kernels, local(): pl.pallas_call(kernel, out_shape=(block, block), in_specs=[pl.BlockSpec(m...  60.6 us
    unnamed x2, local copies, waits for them, and re-layouts  1.35 us

profile of v2, /device:TPU:2, one launch (start us, length us, event | category | flops | bytes accessed | tf_op | source)
XLA Modules:
  0.0 62.6 jit_solution(9044238712235814495)
XLA Ops:
  0.6 60.6 %shard_map.59 = (bf16[80,1152]{1,0:T(8,128)(2,1)S(1)}, bf16[80,1152]{1,0:T(8,128)(2,1)S(1)}) custom-call(bf16[80,1152]{1,0:T(8,128)(2,1)} %image_ref.1, bf16[80,1152]{1,0:T(8,128)(2,1)} %text_ref.1, f32[1152]{0:T(1024)} %image_gain_ref.1, f32[1152]{0:T(1024)} %text_gain_ref.1), custom_call_target="tpu_custom_call" | custom-call | flops 11324620800 | bytes 737280 | tf_op jit(solution)/shard_map/pallas_call | solution.py:437
  61.3 0.7 %copy.8 = bf16[80,1152]{1,0:T(8,128)(2,1)} copy(bf16[80,1152]{1,0:T(8,128)(2,1)S(1)} %get-tuple-element.2) | data formatting | bytes 368640
  61.9 0.7 %copy.9 = bf16[80,1152]{1,0:T(8,128)(2,1)} copy(bf16[80,1152]{1,0:T(8,128)(2,1)S(1)} %get-tuple-element.3) | data formatting | bytes 368640

commit v3 on v2

--- a/solution.py
+++ b/solution.py
@@ -195,104 +195,60 @@
         w[ts, im] = weights
         wt[im, ts] = weights.T
 
+    def text_rows(first, count, first_k=0, count_k=TOTAL, add=False):
+        rows, ks = pl.ds(first, count), pl.ds(first_k, count_k)
+        part = jnp.dot(w[rows, ks], ibuf[ks, :], preferred_element_type=F32)
+        dtext[rows, :] = dtext[rows, :] + part if add else part
+
+    def image_rows(first, count, first_k=0, count_k=TOTAL, add=False):
+        rows, ks = pl.ds(first, count), pl.ds(first_k, count_k)
+        part = jnp.dot(wt[rows, ks], tbuf[ks, :], preferred_element_type=F32)
+        dimage[rows, :] = dimage[rows, :] + part if add else part
+
     whole = (0, ROWS)
-    staged[0].wait()
-    staged[1].wait()
-    ibuf[0:ROWS, :] = embed(image_in, image_gain_in, inorm, ir1, ir2)
-    net.greeted()
-    for part in HALVES:
-        for way in ("z+", "z-"):
-            send_z(0, part, way)
-    send_c(0, whole)
-    staged[2].wait()
-    staged[3].wait()
-    tbuf[0:ROWS, :] = embed(text_in, text_gain_in, tnorm, tr1, tr2)
-    for ways in (("p+", "p-"), ("q+", "q-")):
+
+    def own_image():
+        staged[0].wait()
+        staged[1].wait()
+        ibuf[0:ROWS, :] = embed(image_in, image_gain_in, inorm, ir1, ir2)
+        net.greeted()
         for part in HALVES:
-            for way in ways:
-                send_t(0, 0, part, way)
-
-    for k, part in enumerate(HALVES):
-        wait_i(-1, 0, part)
-        send_z(-1, part, "z+")
-        wait_i(1, 0, part)
-        send_z(1, part, "z-")
-        wait_t(-1, 0, part)
-        if k == 0:
-            send_t(-1, 0, part, "p+")
-        wait_t(1, 0, part)
-        if k == 1:
-            send_t(1, 0, part, "p-")
-        for dp in (-1, 1):
-            send_t(dp, 0, part, "q+")
-            send_t(dp, 0, part, "q-")
-        send_c(1, part)
-        send_c(-1, part)
-    for k, part in enumerate(HALVES):
-        wait_t(0, -1, part)
-        send_t(0, -1, part, "q+")
-        wait_t(0, 1, part)
-        wait_i(-2, 0, part)
-        send_z(-2, part, "z+")
-        wait_i(2, 0, part)
-        send_z(2, part, "z-")
-        wait_t(2, 0, part)
-        send_t(2, 0, part, "q+")
-        send_t(2, 0, part, "q-")
-        send_c(2, part)
-        send_c(-2, part)
-    wait_i(0, 1, whole)
-    for part in HALVES:
-        wait_i(1, 1, part)
-        wait_i(-1, 1, part)
-    tile(0, 256, 0, 256)
-    for part in HALVES:
-        wait_t(1, -1, part)
-        send_t(1, -1, part, "q+")
-        wait_t(-1, 1, part)
-        send_t(-1, 1, part, "q-")
-        wait_i(-3, 0, part)
-        send_z(-3, part, "z+")
-        wait_i(3, 0, part)
-        send_c(3, part)
-        send_c(-3, part)
-        wait_t(1, 1, part)
-        wait_t(-1, -1, part)
-    for part in HALVES:
-        wait_i(2, 1, part)
-        wait_i(-2, 1, part)
-    tile(0, 256, 256, 512)
-    tile(256, 256, 0, 256)
-    for part in HALVES:
-        wait_t(2, 1, part)
-        send_t(2, 1, part, "q-")
-        wait_t(2, -1, part)
-    tile(256, 256, 256, 512)
-    for part in HALVES:
-        wait_i(4, 0, part)
-        send_c(4, part)
-    tile(512, 256, 0, 768)
-    for part in HALVES:
-        wait_i(3, 1, part)
-        wait_i(-3, 1, part)
-    tile(0, 768, 768, 256)
-    for part in HALVES:
-        wait_i(4, 1, part)
-    tile(0, 768, 1024, 256)
-    for part in HALVES:
-        for dp in (0, 1, -1, 2):
-            wait_t(dp, 2, part)
-    tile(768, 512, 768, 512)
-    tile(768, 512, 0, 256)
-    tile(768, 512, 256, 512)
-
-    def text_rows(dq):
-        rows = pl.ds(t_row(0, dq), 4 * ROWS)
-        dtext[rows, :] = jnp.dot(w[rows, :], ibuf[...], preferred_element_type=F32)
-
-    def image_rows(first, count):
-        rows = pl.ds(first * ROWS, count * ROWS)
-        dimage[rows, :] = jnp.dot(wt[rows, :], tbuf[...], preferred_element_type=F32)
+            for way in ("z+", "z-"):
+                send_z(0, part, way)
+        send_c(0, whole)
+
+    def own_text():
+        staged[2].wait()
+        staged[3].wait()
+        tbuf[0:ROWS, :] = embed(text_in, text_gain_in, tnorm, tr1, tr2)
+        for ways in (("p+", "p-"), ("q+", "q-")):
+            for part in HALVES:
+                for way in ways:
+                    send_t(0, 0, part, way)
+
+    def hop_image(dz, k):
+        part = HALVES[k]
+        wait_i(dz, 0, part)
+        if dz in (-1, -2, -3):
+            send_z(dz, part, "z+")
+        if dz in (1, 2):
+            send_z(dz, part, "z-")
+        send_c(dz, part)
+
+    def hop_text(dp, dq, k):
+        part = HALVES[k]
+        wait_t(dp, dq, part)
+        if dq == 0:
+            if dp == -1 and k == 0:
+                send_t(dp, dq, part, "p+")
+            if dp == 1 and k == 1:
+                send_t(dp, dq, part, "p-")
+            send_t(dp, dq, part, "q+")
+            send_t(dp, dq, part, "q-")
+        elif dq == -1 and dp in (0, 1):
+            send_t(dp, dq, part, "q+")
+        elif dq == 1 and dp in (-1, 2):
+            send_t(dp, dq, part, "q-")
 
     slots = {}
 
@@ -346,86 +302,191 @@
         out[...] = total.astype(BF16)
         net.send(("ir", key, first), out, irecv.at[slot("i", key), pl.ds(first, size)], way)
 
-    def join(dp):
-        for first, size in HALVES:
-            rows = pl.ds(t_row(dp, 0) + first, size)
-            dtext[rows, :] = taken_t(dtext[rows, :], dp, 0, (first, size), ("q+", "q-"))
-
-    def pass_t(dp, dq, way, takes=()):
-        for part in HALVES:
-            reduce_t(dp, dq, part, way, takes)
-
-    def pass_i(dz, way, takes=()):
-        for part in HALVES:
-            reduce_i(dz, part, way, takes)
-
-    image_rows(10, 6)
-    for dz in (4, 3, -3):
-        swap(dz)
-    text_rows(2)
-    for dp, way in ((2, "q+"), (1, "q-"), (0, "q+"), (-1, "q-")):
-        pass_t(dp, 2, way)
+    def join(dp, part):
+        first, size = part
+        rows = pl.ds(t_row(dp, 0) + first, size)
+        dtext[rows, :] = taken_t(dtext[rows, :], dp, 0, part, ("q+", "q-"))
+
+    def finish_text():
+        total = dtext[0:ROWS, :]
+        sums = [
+            taken_t(total[first : first + size], 0, 0, (first, size), ("p+", "p-"))
+            for first, size in HALVES
+        ]
+        text_out[...] = embed_back(
+            jnp.concatenate(sums, axis=0), text_gain_in, tnorm, tr1, tr2
+        )
+
+    def finish_image():
+        total = dimage[0:ROWS, :]
+        sums = [
+            taken_i(total[first : first + size], 0, (first, size), ("z-", "z+"))
+            for first, size in HALVES
+        ]
+        image_out[...] = embed_back(
+            jnp.concatenate(sums, axis=0), image_gain_in, inorm, ir1, ir2
+        )
+
+    own_image()
+    own_text()
+    wait_i(0, 1, whole)
+    hop_image(-1, 0)
+    hop_text(-1, 0, 0)
+    hop_text(1, 0, 0)
+    hop_image(1, 0)
+    wait_i(1, 1, HALVES[0])
+    hop_text(1, 0, 1)
+    hop_text(-1, 0, 1)
+    hop_image(-1, 1)
+    wait_i(-1, 1, HALVES[0])
+    hop_image(1, 1)
+    hop_text(0, -1, 0)
+    hop_text(0, 1, 0)
+    wait_i(1, 1, HALVES[1])
+    hop_text(0, -1, 1)
+    hop_text(0, 1, 1)
+    hop_image(-2, 0)
+    wait_i(-1, 1, HALVES[1])
+    hop_text(2, 0, 0)
+    hop_text(-1, 1, 0)
+    hop_image(2, 0)
+    wait_i(2, 1, HALVES[0])
+    hop_image(-2, 1)
+    hop_text(-1, -1, 0)
+    hop_text(1, 1, 0)
+    wait_i(-2, 1, HALVES[0])
+    hop_image(2, 1)
+    hop_text(2, 0, 1)
+    tile(0, 256, 0, 256)
+    hop_text(1, -1, 0)
+    tile(0, 256, 256, 256)
+    wait_i(2, 1, HALVES[1])
+    hop_text(1, 1, 1)
+    hop_text(1, -1, 1)
+    hop_image(-3, 0)
+    wait_i(-2, 1, HALVES[1])
+    tile(0, 256, 512, 256)
+    hop_text(-1, 1, 1)
+    tile(256, 256, 0, 256)
+    hop_text(-1, -1, 1)
+    tile(256, 256, 256, 256)
+    tile(256, 256, 512, 256)
+    hop_image(3, 0)
+    hop_text(2, 1, 0)
+    wait_i(3, 1, HALVES[0])
+    hop_text(0, 2, 0)
+    hop_image(-3, 1)
+    hop_text(0, 2, 1)
+    hop_text(-1, 2, 0)
+    hop_image(3, 1)
+    wait_i(-3, 1, HALVES[0])
+    wait_i(3, 1, HALVES[1])
+    tile(256, 256, 768, 256)
+    hop_text(2, 1, 1)
+    tile(0, 256, 768, 256)
+    hop_text(2, -1, 0)
+    hop_image(4, 0)
+    wait_i(-3, 1, HALVES[1])
+    hop_text(-1, 2, 1)
+    hop_text(2, -1, 1)
+    tile(512, 384, 512, 256)
+    tile(512, 384, 768, 256)
+    tile(512, 384, 0, 256)
+    hop_image(4, 1)
+    wait_i(4, 1, HALVES[0])
+    hop_text(2, 2, 0)
+    tile(512, 384, 256, 256)
+    hop_text(1, 2, 0)
+    hop_text(1, 2, 1)
+    wait_i(4, 1, HALVES[1])
+    tile(0, 256, 1024, 256)
+    hop_text(2, 2, 1)
+    tile(896, 384, 768, 256)
+    tile(896, 384, 0, 256)
+    tile(896, 384, 256, 256)
+    tile(512, 384, 1024, 256)
+    tile(256, 256, 1024, 256)
+    tile(896, 384, 512, 256)
+    tile(896, 384, 1024, 256)
+    image_rows(1120, 160)
+    swap(4)
+    text_rows(960, 320)
+    reduce_t(2, 2, HALVES[0], "q+", ())
+    reduce_t(2, 2, HALVES[1], "q+", ())
+    reduce_t(-1, 2, HALVES[0], "q-", ())
+    reduce_t(-1, 2, HALVES[1], "q-", ())
+    image_rows(800, 320)
+    swap(-3)
     swapped(4)
-    pass_i(4, "z+")
+    reduce_i(4, HALVES[1], "z+", ())
+    reduce_i(4, HALVES[0], "z+", ())
+    swap(3)
+    text_rows(320, 320)
+    reduce_t(1, 1, HALVES[1], "q+", ())
+    reduce_t(1, 2, HALVES[1], "q-", ())
+    reduce_t(1, 2, HALVES[0], "q-", ())
+    swapped(3)
+    reduce_t(-1, 1, HALVES[0], "q+", ())
+    text_rows(640, 320)
     swapped(-3)
-    pass_i(-3, "z-")
-    swapped(3)
-    text_rows(1)
-    pass_t(1, 1, "q+")
-    text_rows(-1)
-    pass_t(2, -1, "q-")
-    for part in HALVES:
-        reduce_t(2, 1, part, "q+", ("q+",))
-        reduce_t(1, -1, part, "q-", ("q-",))
-    pass_t(-1, 1, "q+")
-    pass_t(0, -1, "q-")
-    image_rows(6, 4)
-    for dz in (2, -2):
-        swap(dz)
-    text_rows(0)
-    pass_i(3, "z+", ("z+",))
-    for part in HALVES:
-        reduce_t(0, 1, part, "q+", ("q+",))
-        reduce_t(-1, -1, part, "q-", ("q-",))
+    reduce_i(-3, HALVES[1], "z-", ())
+    reduce_i(-3, HALVES[0], "z-", ())
+    reduce_t(2, -1, HALVES[0], "q-", ())
+    reduce_t(2, 1, HALVES[0], "q+", ("q+",))
+    reduce_t(2, -1, HALVES[1], "q-", ())
+    image_rows(480, 320)
+    reduce_t(2, 1, HALVES[1], "q+", ("q+",))
+    reduce_i(3, HALVES[1], "z+", ("z+",))
+    swap(2)
+    reduce_t(0, 2, HALVES[0], "q+", ())
+    reduce_t(-1, -1, HALVES[0], "q-", ("q-",))
+    reduce_i(3, HALVES[0], "z+", ("z+",))
+    text_rows(0, 320)
+    reduce_t(1, -1, HALVES[1], "q-", ("q-",))
+    reduce_t(1, 1, HALVES[0], "q+", ())
+    reduce_t(1, -1, HALVES[0], "q-", ("q-",))
     swapped(-2)
-    pass_i(-2, "z-", ("z-",))
+    reduce_t(0, 2, HALVES[1], "q+", ())
+    swap(-2)
+    reduce_i(-2, HALVES[1], "z-", ("z-",))
+    image_rows(160, 320)
+    reduce_i(-2, HALVES[0], "z-", ("z-",))
+    swap(1)
+    reduce_t(-1, -1, HALVES[1], "q-", ("q-",))
+    reduce_t(-1, 1, HALVES[1], "q+", ())
+    swap(-1)
     swapped(2)
-    image_rows(2, 4)
-    for dz in (1, -1):
-        swap(dz)
-    join(2)
+    join(2, HALVES[1])
+    join(2, HALVES[0])
+    reduce_t(2, 0, HALVES[1], "p-", ())
     reduce_t(2, 0, HALVES[0], "p+", ())
-    reduce_t(2, 0, HALVES[1], "p-", ())
-    pass_i(2, "z+", ("z+",))
+    reduce_i(2, HALVES[1], "z+", ("z+",))
+    reduce_t(0, -1, HALVES[1], "q-", ())
+    image_rows(0, 160)
+    swap(0)
+    reduce_t(0, 1, HALVES[0], "q+", ("q+",))
+    reduce_t(0, -1, HALVES[0], "q-", ())
+    join(-1, HALVES[0])
     swapped(-1)
-    pass_i(-1, "z-", ("z-",))
+    reduce_i(2, HALVES[0], "z+", ("z+",))
     swapped(1)
-    image_rows(0, 2)
-    swap(0)
-    join(1)
+    join(1, HALVES[1])
+    reduce_i(-1, HALVES[1], "z-", ("z-",))
+    swapped(0)
+    reduce_t(0, 1, HALVES[1], "q+", ("q+",))
+    join(1, HALVES[0])
     reduce_t(1, 0, HALVES[1], "p+", ())
-    join(-1)
+    reduce_i(-1, HALVES[0], "z-", ("z-",))
+    join(-1, HALVES[1])
     reduce_t(-1, 0, HALVES[0], "p-", ())
-    pass_i(1, "z+", ("z+",))
+    reduce_i(1, HALVES[1], "z+", ("z+",))
+    reduce_t(-1, 0, HALVES[1], "p-", ("p-",))
     reduce_t(1, 0, HALVES[0], "p+", ("p+",))
-    reduce_t(-1, 0, HALVES[1], "p-", ("p-",))
-    join(0)
-    swapped(0)
-
-    total = dtext[0:ROWS, :]
-    sums = [
-        taken_t(total[first : first + size], 0, 0, (first, size), ("p+", "p-"))
-        for first, size in HALVES
-    ]
-    text_out[...] = embed_back(jnp.concatenate(sums, axis=0), text_gain_in, tnorm, tr1, tr2)
-    total = dimage[0:ROWS, :]
-    sums = [
-        taken_i(total[first : first + size], 0, (first, size), ("z-", "z+"))
-        for first, size in HALVES
-    ]
-    image_out[...] = embed_back(
-        jnp.concatenate(sums, axis=0), image_gain_in, inorm, ir1, ir2
-    )
+    reduce_i(1, HALVES[0], "z+", ("z+",))
+    join(0, HALVES[0])
+    join(0, HALVES[1])
+    finish_text()
+    finish_image()
     assert len(net.copies) <= N_COPIES, len(net.copies)
     net.finish()
 

time: 63.5 us -> 59.2 us (0.932)
  Pallas kernels: 60.6 us -> 56.4 us
    pallas_call x1, Pallas kernels: 60.6 us -> 56.4 us  [local(): pl.pallas_call(kernel, out_shape=(block, block), in_specs=[pl.BlockSpec(m...]
where the time goes in v3:
time: 59.2 us; the launch traced here: 58.4 us
  Pallas kernels  56.4 us (95%)
  local copies, waits for them, and re-layouts  1.35 us (2%)
  between operations  0.64 us (1%)
    pallas_call x1, Pallas kernels, local(): pl.pallas_call(kernel, out_shape=(block, block), in_specs=[pl.BlockSpec(m...  56.4 us
    unnamed x2, local copies, waits for them, and re-layouts  1.35 us

profile of v3, /device:TPU:2, one launch (start us, length us, event | category | flops | bytes accessed | tf_op | source)
XLA Modules:
  0.0 58.4 jit_solution(17365651638729415660)
XLA Ops:
  0.6 56.4 %shard_map.59 = (bf16[80,1152]{1,0:T(8,128)(2,1)S(1)}, bf16[80,1152]{1,0:T(8,128)(2,1)S(1)}) custom-call(bf16[80,1152]{1,0:T(8,128)(2,1)} %image_ref.1, bf16[80,1152]{1,0:T(8,128)(2,1)} %text_ref.1, f32[1152]{0:T(1024)} %image_gain_ref.1, f32[1152]{0:T(1024)} %text_gain_ref.1), custom_call_target="tpu_custom_call" | custom-call | flops 11324620800 | bytes 737280 | tf_op jit(solution)/shard_map/pallas_call | solution.py:498
  57.1 0.7 %copy.8 = bf16[80,1152]{1,0:T(8,128)(2,1)} copy(bf16[80,1152]{1,0:T(8,128)(2,1)S(1)} %get-tuple-element.2) | data formatting | bytes 368640
  57.7 0.7 %copy.9 = bf16[80,1152]{1,0:T(8,128)(2,1)} copy(bf16[80,1152]{1,0:T(8,128)(2,1)S(1)} %get-tuple-element.3) | data formatting | bytes 368640

commit v4 on v3

--- a/solution.py
+++ b/solution.py
@@ -334,17 +334,17 @@
     hop_text(-1, 0, 0)
     hop_text(1, 0, 0)
     hop_image(1, 0)
-    wait_i(1, 1, HALVES[0])
     hop_text(1, 0, 1)
     hop_text(-1, 0, 1)
+    wait_i(1, 1, HALVES[0])
     hop_image(-1, 1)
-    wait_i(-1, 1, HALVES[0])
     hop_image(1, 1)
     hop_text(0, -1, 0)
     hop_text(0, 1, 0)
-    wait_i(1, 1, HALVES[1])
+    wait_i(-1, 1, HALVES[0])
     hop_text(0, -1, 1)
     hop_text(0, 1, 1)
+    wait_i(1, 1, HALVES[1])
     hop_image(-2, 0)
     wait_i(-1, 1, HALVES[1])
     hop_text(2, 0, 0)
@@ -354,23 +354,21 @@
     hop_image(-2, 1)
     hop_text(-1, -1, 0)
     hop_text(1, 1, 0)
-    wait_i(-2, 1, HALVES[0])
     hop_image(2, 1)
     hop_text(2, 0, 1)
-    tile(0, 256, 0, 256)
+    tile(0, 256, 0, 512)
     hop_text(1, -1, 0)
-    tile(0, 256, 256, 256)
+    wait_i(-2, 1, HALVES[0])
+    hop_text(1, 1, 1)
     wait_i(2, 1, HALVES[1])
-    hop_text(1, 1, 1)
     hop_text(1, -1, 1)
     hop_image(-3, 0)
+    hop_text(-1, 1, 1)
+    tile(256, 256, 0, 512)
+    hop_text(-1, -1, 1)
     wait_i(-2, 1, HALVES[1])
+    tile(256, 256, 512, 256)
     tile(0, 256, 512, 256)
-    hop_text(-1, 1, 1)
-    tile(256, 256, 0, 256)
-    hop_text(-1, -1, 1)
-    tile(256, 256, 256, 256)
-    tile(256, 256, 512, 256)
     hop_image(3, 0)
     hop_text(2, 1, 0)
     wait_i(3, 1, HALVES[0])
@@ -380,109 +378,107 @@
     hop_text(-1, 2, 0)
     hop_image(3, 1)
     wait_i(-3, 1, HALVES[0])
+    hop_text(2, 1, 1)
     wait_i(3, 1, HALVES[1])
     tile(256, 256, 768, 256)
-    hop_text(2, 1, 1)
     tile(0, 256, 768, 256)
+    hop_image(4, 0)
+    hop_text(-1, 2, 1)
     hop_text(2, -1, 0)
-    hop_image(4, 0)
     wait_i(-3, 1, HALVES[1])
-    hop_text(-1, 2, 1)
     hop_text(2, -1, 1)
+    tile(512, 384, 768, 256)
     tile(512, 384, 512, 256)
-    tile(512, 384, 768, 256)
-    tile(512, 384, 0, 256)
+    tile(512, 384, 0, 512)
     hop_image(4, 1)
+    hop_text(1, 2, 0)
+    hop_text(2, 2, 0)
     wait_i(4, 1, HALVES[0])
-    hop_text(2, 2, 0)
-    tile(512, 384, 256, 256)
-    hop_text(1, 2, 0)
     hop_text(1, 2, 1)
+    hop_text(2, 2, 1)
+    tile(896, 384, 0, 512)
+    tile(896, 384, 768, 256)
+    tile(896, 384, 512, 256)
     wait_i(4, 1, HALVES[1])
+    tile(256, 256, 1024, 256)
     tile(0, 256, 1024, 256)
-    hop_text(2, 2, 1)
-    tile(896, 384, 768, 256)
-    tile(896, 384, 0, 256)
-    tile(896, 384, 256, 256)
     tile(512, 384, 1024, 256)
-    tile(256, 256, 1024, 256)
-    tile(896, 384, 512, 256)
     tile(896, 384, 1024, 256)
     image_rows(1120, 160)
     swap(4)
     text_rows(960, 320)
+    reduce_t(-1, 2, HALVES[1], "q-", ())
+    reduce_t(1, 2, HALVES[0], "q-", ())
     reduce_t(2, 2, HALVES[0], "q+", ())
     reduce_t(2, 2, HALVES[1], "q+", ())
+    image_rows(800, 320)
+    swap(3)
+    swapped(4)
+    reduce_i(4, HALVES[0], "z+", ())
+    reduce_t(1, 2, HALVES[1], "q-", ())
+    text_rows(320, 320)
+    reduce_t(-1, 1, HALVES[0], "q+", ())
+    reduce_t(1, 1, HALVES[0], "q+", ())
+    reduce_i(4, HALVES[1], "z+", ())
+    swap(-3)
     reduce_t(-1, 2, HALVES[0], "q-", ())
-    reduce_t(-1, 2, HALVES[1], "q-", ())
-    image_rows(800, 320)
-    swap(-3)
-    swapped(4)
-    reduce_i(4, HALVES[1], "z+", ())
-    reduce_i(4, HALVES[0], "z+", ())
-    swap(3)
-    text_rows(320, 320)
-    reduce_t(1, 1, HALVES[1], "q+", ())
-    reduce_t(1, 2, HALVES[1], "q-", ())
-    reduce_t(1, 2, HALVES[0], "q-", ())
-    swapped(3)
-    reduce_t(-1, 1, HALVES[0], "q+", ())
     text_rows(640, 320)
     swapped(-3)
     reduce_i(-3, HALVES[1], "z-", ())
     reduce_i(-3, HALVES[0], "z-", ())
+    reduce_t(2, -1, HALVES[1], "q-", ())
+    reduce_t(2, 1, HALVES[0], "q+", ("q+",))
     reduce_t(2, -1, HALVES[0], "q-", ())
-    reduce_t(2, 1, HALVES[0], "q+", ("q+",))
-    reduce_t(2, -1, HALVES[1], "q-", ())
     image_rows(480, 320)
+    swapped(3)
+    reduce_i(3, HALVES[0], "z+", ("z+",))
+    swap(2)
     reduce_t(2, 1, HALVES[1], "q+", ("q+",))
+    reduce_t(1, -1, HALVES[1], "q-", ("q-",))
+    reduce_t(-1, 1, HALVES[1], "q+", ())
+    reduce_t(-1, -1, HALVES[1], "q-", ("q-",))
+    text_rows(0, 320)
+    reduce_t(-1, -1, HALVES[0], "q-", ("q-",))
     reduce_i(3, HALVES[1], "z+", ("z+",))
-    swap(2)
     reduce_t(0, 2, HALVES[0], "q+", ())
-    reduce_t(-1, -1, HALVES[0], "q-", ("q-",))
-    reduce_i(3, HALVES[0], "z+", ("z+",))
-    text_rows(0, 320)
-    reduce_t(1, -1, HALVES[1], "q-", ("q-",))
-    reduce_t(1, 1, HALVES[0], "q+", ())
+    reduce_t(0, 2, HALVES[1], "q+", ())
+    swap(-2)
     reduce_t(1, -1, HALVES[0], "q-", ("q-",))
     swapped(-2)
-    reduce_t(0, 2, HALVES[1], "q+", ())
-    swap(-2)
     reduce_i(-2, HALVES[1], "z-", ("z-",))
     image_rows(160, 320)
     reduce_i(-2, HALVES[0], "z-", ("z-",))
     swap(1)
-    reduce_t(-1, -1, HALVES[1], "q-", ("q-",))
-    reduce_t(-1, 1, HALVES[1], "q+", ())
     swap(-1)
+    reduce_t(1, 1, HALVES[1], "q+", ())
+    reduce_t(0, -1, HALVES[0], "q-", ())
+    image_rows(0, 160)
     swapped(2)
     join(2, HALVES[1])
+    reduce_i(2, HALVES[0], "z+", ("z+",))
+    swap(0)
     join(2, HALVES[0])
     reduce_t(2, 0, HALVES[1], "p-", ())
     reduce_t(2, 0, HALVES[0], "p+", ())
+    join(-1, HALVES[1])
+    reduce_t(0, -1, HALVES[1], "q-", ())
     reduce_i(2, HALVES[1], "z+", ("z+",))
-    reduce_t(0, -1, HALVES[1], "q-", ())
-    image_rows(0, 160)
-    swap(0)
+    swapped(-1)
+    swapped(1)
     reduce_t(0, 1, HALVES[0], "q+", ("q+",))
-    reduce_t(0, -1, HALVES[0], "q-", ())
     join(-1, HALVES[0])
-    swapped(-1)
-    reduce_i(2, HALVES[0], "z+", ("z+",))
-    swapped(1)
-    join(1, HALVES[1])
+    reduce_t(-1, 0, HALVES[0], "p-", ())
     reduce_i(-1, HALVES[1], "z-", ("z-",))
     swapped(0)
     reduce_t(0, 1, HALVES[1], "q+", ("q+",))
     join(1, HALVES[0])
+    reduce_i(-1, HALVES[0], "z-", ("z-",))
+    join(1, HALVES[1])
     reduce_t(1, 0, HALVES[1], "p+", ())
-    reduce_i(-1, HALVES[0], "z-", ("z-",))
-    join(-1, HALVES[1])
-    reduce_t(-1, 0, HALVES[0], "p-", ())
+    reduce_i(1, HALVES[0], "z+", ("z+",))
+    reduce_t(1, 0, HALVES[0], "p+", ("p+",))
+    reduce_t(-1, 0, HALVES[1], "p-", ("p-",))
     reduce_i(1, HALVES[1], "z+", ("z+",))
-    reduce_t(-1, 0, HALVES[1], "p-", ("p-",))
-    reduce_t(1, 0, HALVES[0], "p+", ("p+",))
-    reduce_i(1, HALVES[0], "z+", ("z+",))
     join(0, HALVES[0])
     join(0, HALVES[1])
     finish_text()

time: 59.2 us -> 60.4 us (1.020)
  Pallas kernels: 56.4 us -> 57.4 us
    pallas_call x1, Pallas kernels: 56.4 us -> 57.4 us  [local(): pl.pallas_call(kernel, out_shape=(block, block), in_specs=[pl.BlockSpec(m...]
where the time goes in v4:
time: 60.4 us; the launch traced here: 59.4 us
  Pallas kernels  57.4 us (95%)
  local copies, waits for them, and re-layouts  1.35 us (2%)
  between operations  0.64 us (1%)
    pallas_call x1, Pallas kernels, local(): pl.pallas_call(kernel, out_shape=(block, block), in_specs=[pl.BlockSpec(m...  57.4 us
    unnamed x2, local copies, waits for them, and re-layouts  1.35 us

profile of v4, /device:TPU:2, one launch (start us, length us, event | category | flops | bytes accessed | tf_op | source)
XLA Modules:
  0.0 59.4 jit_solution(9107778002031189819)
XLA Ops:
  0.6 57.4 %shard_map.59 = (bf16[80,1152]{1,0:T(8,128)(2,1)S(1)}, bf16[80,1152]{1,0:T(8,128)(2,1)S(1)}) custom-call(bf16[80,1152]{1,0:T(8,128)(2,1)} %image_ref.1, bf16[80,1152]{1,0:T(8,128)(2,1)} %text_ref.1, f32[1152]{0:T(1024)} %image_gain_ref.1, f32[1152]{0:T(1024)} %text_gain_ref.1), custom_call_target="tpu_custom_call" | custom-call | flops 11324620800 | bytes 737280 | tf_op jit(solution)/shard_map/pallas_call | solution.py:494
  58.1 0.7 %copy.8 = bf16[80,1152]{1,0:T(8,128)(2,1)} copy(bf16[80,1152]{1,0:T(8,128)(2,1)S(1)} %get-tuple-element.2) | data formatting | bytes 368640
  58.8 0.7 %copy.9 = bf16[80,1152]{1,0:T(8,128)(2,1)} copy(bf16[80,1152]{1,0:T(8,128)(2,1)S(1)} %get-tuple-element.3) | data formatting | bytes 368640

commit v5 on v3

--- a/solution.py
+++ b/solution.py
@@ -491,11 +491,22 @@
     net.finish()
 
 
+def store(image_ref, text_ref, image_out, text_out, sems):
+    copies = [
+        pltpu.make_async_copy(image_ref, image_out, sems.at[0]),
+        pltpu.make_async_copy(text_ref, text_out, sems.at[1]),
+    ]
+    for copy in copies:
+        copy.start()
+    for copy in copies:
+        copy.wait()
+
+
 def local(image_feats, text_feats, image_gain, text_gain):
     vmem = pl.BlockSpec(memory_space=pltpu.VMEM)
     block = pltpu.VMEM((ROWS, WIDTH), BF16)
     flops = 6 * TOTAL * TOTAL * WIDTH
-    return pl.pallas_call(
+    results = pl.pallas_call(
         kernel,
         out_shape=(block, block),
         in_specs=[pl.BlockSpec(memory_space=pl.ANY)] * 4,
@@ -534,6 +545,15 @@
             flops=flops, bytes_accessed=4 * ROWS * WIDTH * 2, transcendentals=TOTAL * TOTAL
         ),
     )(image_feats, text_feats, image_gain, text_gain)
+    block = jax.ShapeDtypeStruct((ROWS, WIDTH), BF16)
+    anywhere = pl.BlockSpec(memory_space=pl.ANY)
+    return pl.pallas_call(
+        store,
+        out_shape=(block, block),
+        in_specs=[anywhere] * 2,
+        out_specs=(anywhere, anywhere),
+        scratch_shapes=[pltpu.SemaphoreType.DMA((2,))],
+    )(*results)
 
 
 def solution(mesh):

time: 59.2 us -> 71.6 us (1.21)
  Pallas kernels: 56.4 us -> 68.7 us
    pallas_call x0 -> x1, Pallas kernels: none -> 12.3 us  [local(): pl.pallas_call(store, out_shape=(block, block), in_specs=[anywhere] * 2,...]
where the time goes in v5:
time: 71.6 us; the launch traced here: 70.8 us
  Pallas kernels  68.7 us (96%)
  local copies, waits for them, and re-layouts  1.32 us (2%)
  between operations  0.81 us (1%)
    pallas_call x1, Pallas kernels, local(): pl.pallas_call(kernel, out_shape=(block, block), in_specs=[pl.BlockSpec(m...  56.4 us
    pallas_call x1, Pallas kernels, local(): pl.pallas_call(store, out_shape=(block, block), in_specs=[anywhere] * 2,...  12.3 us

profile of v5, /device:TPU:2, one launch (start us, length us, event | category | flops | bytes accessed | tf_op | source)
XLA Modules:
  0.0 70.8 jit_solution(15338635249918051543)
XLA Ops:
  0.6 56.4 %shard_map.59 = (bf16[80,1152]{1,0:T(8,128)(2,1)S(1)}, bf16[80,1152]{1,0:T(8,128)(2,1)S(1)}) custom-call(bf16[80,1152]{1,0:T(8,128)(2,1)} %image_ref.1, bf16[80,1152]{1,0:T(8,128)(2,1)} %text_ref.1, f32[1152]{0:T(1024)} %image_gain_ref.1, f32[1152]{0:T(1024)} %text_gain_ref.1), custom_call_target="tpu_custom_call" | custom-call | flops 11324620800 | bytes 737280 | tf_op jit(solution)/shard_map/pallas_call | solution.py:509
  57.1 0.0 copy-start
  57.1 0.7 copy-done
  57.7 0.0 copy-start.1
  57.7 0.7 copy-done.1
  58.4 12.3 %shard_map.60 = (bf16[80,1152]{1,0:T(8,128)(2,1)}, bf16[80,1152]{1,0:T(8,128)(2,1)}) custom-call(bf16[80,1152]{1,0:T(8,128)(2,1)} %copy-done, bf16[80,1152]{1,0:T(8,128)(2,1)} %copy-done.1), custom_call_target="tpu_custom_call" | custom-call | tf_op jit(solution)/shard_map/pallas_call | solution.py:550
Async XLA Ops:
  57.1 0.7 copy-start
  57.7 0.7 copy-start.1

commit v6 on v4

--- a/solution.py
+++ b/solution.py
@@ -356,128 +356,132 @@
     hop_text(1, 1, 0)
     hop_image(2, 1)
     hop_text(2, 0, 1)
-    tile(0, 256, 0, 512)
+    tile(0, 256, 256, 256)
     hop_text(1, -1, 0)
     wait_i(-2, 1, HALVES[0])
+    tile(0, 256, 0, 256)
     hop_text(1, 1, 1)
     wait_i(2, 1, HALVES[1])
     hop_text(1, -1, 1)
     hop_image(-3, 0)
     hop_text(-1, 1, 1)
-    tile(256, 256, 0, 512)
-    hop_text(-1, -1, 1)
+    tile(256, 256, 256, 256)
     wait_i(-2, 1, HALVES[1])
     tile(256, 256, 512, 256)
+    tile(256, 256, 0, 256)
+    hop_image(3, 0)
+    hop_text(-1, -1, 1)
     tile(0, 256, 512, 256)
-    hop_image(3, 0)
     hop_text(2, 1, 0)
     wait_i(3, 1, HALVES[0])
     hop_text(0, 2, 0)
     hop_image(-3, 1)
+    hop_text(-1, 2, 0)
     hop_text(0, 2, 1)
-    hop_text(-1, 2, 0)
     hop_image(3, 1)
     wait_i(-3, 1, HALVES[0])
     hop_text(2, 1, 1)
     wait_i(3, 1, HALVES[1])
     tile(256, 256, 768, 256)
+    hop_text(2, -1, 0)
     tile(0, 256, 768, 256)
     hop_image(4, 0)
     hop_text(-1, 2, 1)
-    hop_text(2, -1, 0)
     wait_i(-3, 1, HALVES[1])
     hop_text(2, -1, 1)
+    tile(512, 384, 256, 256)
+    tile(512, 384, 0, 256)
     tile(512, 384, 768, 256)
+    hop_image(4, 1)
     tile(512, 384, 512, 256)
-    tile(512, 384, 0, 512)
-    hop_image(4, 1)
     hop_text(1, 2, 0)
+    wait_i(4, 1, HALVES[0])
     hop_text(2, 2, 0)
-    wait_i(4, 1, HALVES[0])
     hop_text(1, 2, 1)
     hop_text(2, 2, 1)
-    tile(896, 384, 0, 512)
+    tile(896, 384, 256, 256)
+    tile(896, 384, 0, 256)
     tile(896, 384, 768, 256)
     tile(896, 384, 512, 256)
     wait_i(4, 1, HALVES[1])
     tile(256, 256, 1024, 256)
+    tile(896, 384, 1024, 256)
+    tile(512, 384, 1024, 256)
     tile(0, 256, 1024, 256)
-    tile(512, 384, 1024, 256)
-    tile(896, 384, 1024, 256)
     image_rows(1120, 160)
     swap(4)
     text_rows(960, 320)
+    reduce_t(-1, 2, HALVES[0], "q-", ())
     reduce_t(-1, 2, HALVES[1], "q-", ())
     reduce_t(1, 2, HALVES[0], "q-", ())
     reduce_t(2, 2, HALVES[0], "q+", ())
     reduce_t(2, 2, HALVES[1], "q+", ())
     image_rows(800, 320)
-    swap(3)
     swapped(4)
     reduce_i(4, HALVES[0], "z+", ())
-    reduce_t(1, 2, HALVES[1], "q-", ())
+    swap(3)
     text_rows(320, 320)
     reduce_t(-1, 1, HALVES[0], "q+", ())
-    reduce_t(1, 1, HALVES[0], "q+", ())
+    swap(-3)
+    reduce_t(1, 1, HALVES[1], "q+", ())
     reduce_i(4, HALVES[1], "z+", ())
-    swap(-3)
-    reduce_t(-1, 2, HALVES[0], "q-", ())
     text_rows(640, 320)
+    reduce_t(2, -1, HALVES[1], "q-", ())
     swapped(-3)
     reduce_i(-3, HALVES[1], "z-", ())
+    reduce_t(2, -1, HALVES[0], "q-", ())
+    reduce_t(2, 1, HALVES[0], "q+", ("q+",))
     reduce_i(-3, HALVES[0], "z-", ())
-    reduce_t(2, -1, HALVES[1], "q-", ())
-    reduce_t(2, 1, HALVES[0], "q+", ("q+",))
-    reduce_t(2, -1, HALVES[0], "q-", ())
+    reduce_t(1, 2, HALVES[1], "q-", ())
     image_rows(480, 320)
     swapped(3)
     reduce_i(3, HALVES[0], "z+", ("z+",))
     swap(2)
+    swap(-2)
     reduce_t(2, 1, HALVES[1], "q+", ("q+",))
-    reduce_t(1, -1, HALVES[1], "q-", ("q-",))
-    reduce_t(-1, 1, HALVES[1], "q+", ())
+    reduce_t(1, 1, HALVES[0], "q+", ())
+    reduce_t(1, -1, HALVES[0], "q-", ("q-",))
+    image_rows(160, 320)
+    reduce_i(3, HALVES[1], "z+", ("z+",))
+    swap(-1)
+    reduce_t(0, 2, HALVES[0], "q+", ())
     reduce_t(-1, -1, HALVES[1], "q-", ("q-",))
-    text_rows(0, 320)
+    reduce_t(0, 2, HALVES[1], "q+", ())
     reduce_t(-1, -1, HALVES[0], "q-", ("q-",))
-    reduce_i(3, HALVES[1], "z+", ("z+",))
-    reduce_t(0, 2, HALVES[0], "q+", ())
-    reduce_t(0, 2, HALVES[1], "q+", ())
-    swap(-2)
-    reduce_t(1, -1, HALVES[0], "q-", ("q-",))
     swapped(-2)
     reduce_i(-2, HALVES[1], "z-", ("z-",))
-    image_rows(160, 320)
+    text_rows(0, 320)
     reduce_i(-2, HALVES[0], "z-", ("z-",))
+    join(2, HALVES[0])
+    swapped(2)
+    reduce_t(-1, 1, HALVES[1], "q+", ())
     swap(1)
-    swap(-1)
-    reduce_t(1, 1, HALVES[1], "q+", ())
-    reduce_t(0, -1, HALVES[0], "q-", ())
     image_rows(0, 160)
-    swapped(2)
+    reduce_t(1, -1, HALVES[1], "q-", ("q-",))
     join(2, HALVES[1])
     reduce_i(2, HALVES[0], "z+", ("z+",))
+    reduce_t(2, 0, HALVES[0], "p+", ())
+    reduce_t(2, 0, HALVES[1], "p-", ())
+    reduce_t(0, -1, HALVES[1], "q-", ())
+    reduce_t(0, -1, HALVES[0], "q-", ())
+    swapped(1)
     swap(0)
-    join(2, HALVES[0])
-    reduce_t(2, 0, HALVES[1], "p-", ())
-    reduce_t(2, 0, HALVES[0], "p+", ())
-    join(-1, HALVES[1])
-    reduce_t(0, -1, HALVES[1], "q-", ())
+    join(1, HALVES[0])
     reduce_i(2, HALVES[1], "z+", ("z+",))
     swapped(-1)
-    swapped(1)
+    reduce_i(-1, HALVES[1], "z-", ("z-",))
     reduce_t(0, 1, HALVES[0], "q+", ("q+",))
-    join(-1, HALVES[0])
-    reduce_t(-1, 0, HALVES[0], "p-", ())
-    reduce_i(-1, HALVES[1], "z-", ("z-",))
     swapped(0)
     reduce_t(0, 1, HALVES[1], "q+", ("q+",))
-    join(1, HALVES[0])
+    join(-1, HALVES[0])
     reduce_i(-1, HALVES[0], "z-", ("z-",))
+    join(-1, HALVES[1])
+    reduce_t(-1, 0, HALVES[0], "p-", ())
     join(1, HALVES[1])
     reduce_t(1, 0, HALVES[1], "p+", ())
     reduce_i(1, HALVES[0], "z+", ("z+",))
+    reduce_t(-1, 0, HALVES[1], "p-", ("p-",))
     reduce_t(1, 0, HALVES[0], "p+", ("p+",))
-    reduce_t(-1, 0, HALVES[1], "p-", ("p-",))
     reduce_i(1, HALVES[1], "z+", ("z+",))
     join(0, HALVES[0])
     join(0, HALVES[1])

time: 60.4 us -> 60.5 us (level)
  no operation moved by 1% of the time
where the time goes in v6:
time: 60.5 us; the launch traced here: 60 us
  Pallas kernels  58 us (96%)
  local copies, waits for them, and re-layouts  1.35 us (2%)
  between operations  0.64 us (1%)
    pallas_call x1, Pallas kernels, local(): pl.pallas_call(kernel, out_shape=(block, block), in_specs=[pl.BlockSpec(m...  58 us
    unnamed x2, local copies, waits for them, and re-layouts  1.35 us

profile of v6, /device:TPU:2, one launch (start us, length us, event | category | flops | bytes accessed | tf_op | source)
XLA Modules:
  0.0 60.0 jit_solution(17950992497439494519)
XLA Ops:
  0.6 58.0 %shard_map.59 = (bf16[80,1152]{1,0:T(8,128)(2,1)S(1)}, bf16[80,1152]{1,0:T(8,128)(2,1)S(1)}) custom-call(bf16[80,1152]{1,0:T(8,128)(2,1)} %image_ref.1, bf16[80,1152]{1,0:T(8,128)(2,1)} %text_ref.1, f32[1152]{0:T(1024)} %image_gain_ref.1, f32[1152]{0:T(1024)} %text_gain_ref.1), custom_call_target="tpu_custom_call" | custom-call | flops 11324620800 | bytes 737280 | tf_op jit(solution)/shard_map/pallas_call | solution.py:498
  58.7 0.7 %copy.8 = bf16[80,1152]{1,0:T(8,128)(2,1)} copy(bf16[80,1152]{1,0:T(8,128)(2,1)S(1)} %get-tuple-element.2) | data formatting | bytes 368640
  59.3 0.7 %copy.9 = bf16[80,1152]{1,0:T(8,128)(2,1)} copy(bf16[80,1152]{1,0:T(8,128)(2,1)S(1)} %get-tuple-element.3) | data formatting | bytes 368640
